TPU v7x, 32 devices: a whole 2x2x4 slice. The times are simulated.
32 devices in a mesh: groups: 2 (over y), tm: 4 (over z), tok: 4 (over x, core).
Axes of the slice: x: 2, y: 2, z: 4, core: 2. Of those that a mesh axis runs over, the one named last changes fastest.
Arguments:
- queries: bfloat16 [8, 4096, 2048], P(('groups', 'tm'), 'tok'), parts along dimension 0, may hold values from -6 to 6
- keys: bfloat16 [8, 4096, 2048], P(('groups', 'tm'), 'tok'), parts along dimension 0, may hold values from -6 to 6
- values: bfloat16 [8, 4096, 2048], P(('groups', 'tm'), 'tok'), parts along dimension 0, may hold values from -6 to 6
- block_index: int32 [8, 32, 12], P(('groups', 'tm')), parts along dimension 0, may hold values from 0 to 31, all different within a row
- norm_gain: bfloat16 [2048], P('tok'), may hold values from 0.25 to 1.75
- out_weight: bfloat16 [2048, 2048], P('tok'), may hold values from -0.125 to 0.125
Outputs:
- projected: bfloat16 [8, 4096, 2048], P(('groups', 'tm'), 'tok'), parts along dimension 0
There are 2 independent parts, one for each index of `groups`. A program takes and returns all parts, laid end to end along the dimension named above; an argument that names none is the same for every part. Nothing has to cross between parts.
Inputs may be any that keep to these rules, and one draw needn't show every extreme that they name: block_index[t, b, :] holds 12 different block numbers of frame t; every block number appears somewhere.
All inputs are finite; a program needn't handle non-finite values.
Results may differ from a plain program's by a relative error of at most 0.0058.
Values may be sent and summed in bfloat16 or wider, within the bound.
A program may use at most 128 MiB of HBM per device.

v0:
```python
import jax
import jax.numpy as jnp
from jax import lax
from jax.sharding import PartitionSpec as P

HEAD_DIM = 128
BLK = 128
KBLK = 12


def on_device(queries, keys, values, block_index, norm_gain, out_weight):
    frame_count, tok_rows, model_width = queries.shape
    head_total = model_width // HEAD_DIM

    def split_heads(tensor):
        return tensor.reshape(frame_count, tok_rows, head_total, HEAD_DIM)

    q_heads, k_heads, v_heads = (
        lax.all_to_all(split_heads(queries), "tok", split_axis=2, concat_axis=1, tiled=True),
        lax.all_to_all(split_heads(keys), "tok", split_axis=2, concat_axis=1, tiled=True),
        lax.all_to_all(split_heads(values), "tok", split_axis=2, concat_axis=1, tiled=True),
    )
    frame_tokens = q_heads.shape[1]
    head_local = q_heads.shape[2]
    local_state = jnp.einsum("fthc,fthd->hcd", k_heads, v_heads, preferred_element_type=jnp.float32)
    my_section = lax.axis_index("tm")
    piece = lax.all_gather(local_state[None], "tm", axis=0, tiled=True)
    section_ids = jnp.arange(piece.shape[0], dtype=jnp.int32)
    keep = (section_ids < my_section).astype(jnp.float32)
    prefix = jnp.sum(piece * keep[:, None, None, None], axis=0)
    prefix_low = prefix.astype(jnp.bfloat16)
    gain = norm_gain.astype(jnp.float32).reshape(head_local, HEAD_DIM)
    block_count = frame_tokens // BLK
    group_count = block_count // 4
    q_frames = q_heads.reshape(frame_count, group_count, 4, BLK, head_local, HEAD_DIM)
    k_frames = k_heads.reshape(frame_count, block_count, BLK, head_local, HEAD_DIM)
    v_frames = v_heads.reshape(frame_count, block_count, BLK, head_local, HEAD_DIM)
    index_frames = block_index.reshape(frame_count, group_count, 4, KBLK)
    block_ids = jnp.arange(block_count, dtype=jnp.int32)

    def per_frame(frame_item):
        q_frame, index_frame, k_frame, v_frame = frame_item

        def attend(item):
            q_part, chosen = item
            selector = (chosen[:, :, None] == block_ids[None, None, :]).astype(jnp.bfloat16)
            k_sel = jnp.einsum(
                "qkn,njhc->qkjhc", selector, k_frame, preferred_element_type=jnp.float32
            ).astype(jnp.bfloat16)
            v_sel = jnp.einsum(
                "qkn,njhc->qkjhc", selector, v_frame, preferred_element_type=jnp.float32
            ).astype(jnp.bfloat16)
            weight = jnp.einsum(
                "qbhc,qkjhc->qhbkj", q_part, k_sel, preferred_element_type=jnp.float32
            ).astype(jnp.bfloat16)
            intra = jnp.einsum(
                "qhbkj,qkjhd->qbhd", weight, v_sel, preferred_element_type=jnp.float32
            )
            inter = jnp.einsum(
                "qbhc,hcd->qbhd", q_part, prefix_low, preferred_element_type=jnp.float32
            )
            mixed = intra + inter
            scale = lax.rsqrt(jnp.mean(mixed * mixed, axis=-1, keepdims=True) + 1e-06)
            return (mixed * scale * gain).astype(jnp.bfloat16)

        return lax.map(attend, (q_frame, index_frame))

    attended = lax.map(per_frame, (q_frames, index_frames, k_frames, v_frames))
    attended = attended.reshape(frame_count, frame_tokens, head_local, HEAD_DIM)
    returned = lax.all_to_all(attended, "tok", split_axis=1, concat_axis=2, tiled=True)
    token_major = returned.reshape(frame_count, returned.shape[1], head_total * HEAD_DIM)
    total = jnp.einsum(
        "ftc,cd->ftd",
        token_major,
        lax.all_gather(out_weight, "tok", axis=0, tiled=True),
        preferred_element_type=jnp.float32,
    )
    return total.astype(jnp.bfloat16)


def solution(mesh):
    in_specs = (
        P(("groups", "tm"), "tok", None),
        P(("groups", "tm"), "tok", None),
        P(("groups", "tm"), "tok", None),
        P(("groups", "tm"), None, None),
        P("tok"),
        P("tok", None),
    )
    out_specs = P(("groups", "tm"), "tok", None)
    return jax.shard_map(
        on_device, mesh=mesh, in_specs=in_specs, out_specs=out_specs, check_vma=False
    )
```

profile of v0, /device:TPU:1, one launch (start us, length us, event | category | flops | bytes accessed | tf_op | source)
XLA Modules:
  0.0 529.9 jit_solution(4629113330489028375)
XLA Ops:
  24.2 41.3 %all-to-all-done.2 = bf16[1,1024,16,128]{1,3,0,2:T(8,128)(2,1)} async-done(((bf16[1,1024,16,128]{1,3,0,2:T(8,128)(2,1)}), bf16[1,1024,16,128]{1,3,0,2:T(8,128)(2,1)}, u32[]{:S(2)}, u32[]{:S(2)}) %all-to-all-start.2) | async-done | bytes 4194336 | tf_op jit(solution)/shard_map/all_to_all | solution.py:20
  78.0 41.0 %all-to-all-done = bf16[1,1024,16,128]{1,3,0,2:T(8,128)(2,1)} async-done(((bf16[1,1024,16,128]{1,3,0,2:T(8,128)(2,1)}), bf16[1,1024,16,128]{1,3,0,2:T(8,128)(2,1)}, u32[]{:S(2)}, u32[]{:S(2)}) %all-to-all-start) | async-done | bytes 4194336 | tf_op jit(solution)/shard_map/all_to_all | solution.py:21
  131.0 7.8 %copy.92 = bf16[1,4,1024,4,128]{2,1,4,3,0:T(4,128)(2,1)} copy(bf16[1,4,1024,4,128]{4,2,3,1,0:T(8,128)(2,1)} %bitcast.101) | data formatting | bytes 8388608 | tf_op jit(solution)/shard_map/all_to_all | solution.py:20
  138.8 7.7 %reshape.60 = bf16[4096,4,128]{0,2,1:T(8,128)(2,1)} reshape(bf16[1,4,1024,4,128]{2,1,4,3,0:T(4,128)(2,1)} %copy.92) | data formatting | bytes 8388608 | tf_op jit(solution)/shard_map/reshape.8
  173.1 6.4 %copy.86 = bf16[1,1024,16,128]{3,1,2,0:T(8,128)(2,1)} copy(bf16[1,1024,16,128]{1,3,0,2:T(8,128)(2,1)} %all-to-all-done.1) | data formatting | bytes 8388608 | tf_op jit(solution)/shard_map/all_to_all | solution.py:19
  190.9 252.8 %while.18 = (s32[]{:T(128)}, bf16[8,4,128,4,128]{4,2,1,0,3:T(8,128)(2,1)}, s32[8,4,12]{2,1,0:T(4,128)S(1)}, bf16[32,128,4,128]{3,0,2,1:T(8,128)(2,1)}, bf16[8,4,...) while((s32[]{:T(128)}, ...), condition=%wide.region_3.4_spmd.clone, body=%wide.region_1.3_spmd.clone.sunk | while | flops 2091389952 | bytes 62558588 | solution.py:66
  190.9 8.7 %convolution_convert_fusion.4 = bf16[4,12,128,4,128]{4,1,3,2,0:T(8,128)(2,1)} fusion(bf16[32,128,4,128]{3,0,2,1:T(8,128)(2,1)} %get-tuple-element.232, s32[4,12]{1,0:T(4,128)S(1)} %dynamic-slice_bitcast_fusion.2), kind=kOutput, calls=%fused_computation.1.clone.1 | convolution fusion | flops 204473856 | bytes 10485952 | tf_op jit(solution)/shard_map/while/body/eval_jaxpr/while/body/eval_jaxpr/qkn,njhc->qkjhc/dot_general | solution.py:47
  205.3 15.0 %fusion.57 = f32[4,128,4,128]{1,3,2,0:T(8,128)S(1)} fusion(bf16[4,12,128,4,128]{4,1,3,2,0:T(8,128)(2,1)} %convolution_convert_fusion.4, bf16[4,12,128,4,128]{4,1,3,2,0:T(8,128)(2,1)} %convolution_convert_fusion.5, bf16[8,4,128,4,128]{4,2,1,0,3:T(8,128)(2,1)} %get-tuple-element.231, s32[]{:T(128)} %get-tuple-element.218), kind=kOutput, calls=%fused_computation.10.clone.1 | convolution fusion | flops 1613758464 | bytes 18350592 | tf_op jit(solution)/shard_map/while/body/eval_jaxpr/while/body/eval_jaxpr/qhbkj,qkjhd->qbhd/dot_general | solution.py:56
  223.1 8.0 %convolution_convert_fusion.4 = bf16[4,12,128,4,128]{4,1,3,2,0:T(8,128)(2,1)} fusion(bf16[32,128,4,128]{3,0,2,1:T(8,128)(2,1)} %get-tuple-element.232, s32[4,12]{1,0:T(4,128)S(1)} %dynamic-slice_bitcast_fusion.2), kind=kOutput, calls=%fused_computation.1.clone.1 | convolution fusion | flops 204473856 | bytes 10485952 | tf_op jit(solution)/shard_map/while/body/eval_jaxpr/while/body/eval_jaxpr/qkn,njhc->qkjhc/dot_general | solution.py:47
  236.8 15.0 %fusion.57 = f32[4,128,4,128]{1,3,2,0:T(8,128)S(1)} fusion(bf16[4,12,128,4,128]{4,1,3,2,0:T(8,128)(2,1)} %convolution_convert_fusion.4, bf16[4,12,128,4,128]{4,1,3,2,0:T(8,128)(2,1)} %convolution_convert_fusion.5, bf16[8,4,128,4,128]{4,2,1,0,3:T(8,128)(2,1)} %get-tuple-element.231, s32[]{:T(128)} %get-tuple-element.218), kind=kOutput, calls=%fused_computation.10.clone.1 | convolution fusion | flops 1613758464 | bytes 18350592 | tf_op jit(solution)/shard_map/while/body/eval_jaxpr/while/body/eval_jaxpr/qhbkj,qkjhd->qbhd/dot_general | solution.py:56
  254.7 8.0 %convolution_convert_fusion.4 = bf16[4,12,128,4,128]{4,1,3,2,0:T(8,128)(2,1)} fusion(bf16[32,128,4,128]{3,0,2,1:T(8,128)(2,1)} %get-tuple-element.232, s32[4,12]{1,0:T(4,128)S(1)} %dynamic-slice_bitcast_fusion.2), kind=kOutput, calls=%fused_computation.1.clone.1 | convolution fusion | flops 204473856 | bytes 10485952 | tf_op jit(solution)/shard_map/while/body/eval_jaxpr/while/body/eval_jaxpr/qkn,njhc->qkjhc/dot_general | solution.py:47
  268.4 15.0 %fusion.57 = f32[4,128,4,128]{1,3,2,0:T(8,128)S(1)} fusion(bf16[4,12,128,4,128]{4,1,3,2,0:T(8,128)(2,1)} %convolution_convert_fusion.4, bf16[4,12,128,4,128]{4,1,3,2,0:T(8,128)(2,1)} %convolution_convert_fusion.5, bf16[8,4,128,4,128]{4,2,1,0,3:T(8,128)(2,1)} %get-tuple-element.231, s32[]{:T(128)} %get-tuple-element.218), kind=kOutput, calls=%fused_computation.10.clone.1 | convolution fusion | flops 1613758464 | bytes 18350592 | tf_op jit(solution)/shard_map/while/body/eval_jaxpr/while/body/eval_jaxpr/qhbkj,qkjhd->qbhd/dot_general | solution.py:56
  286.2 8.0 %convolution_convert_fusion.4 = bf16[4,12,128,4,128]{4,1,3,2,0:T(8,128)(2,1)} fusion(bf16[32,128,4,128]{3,0,2,1:T(8,128)(2,1)} %get-tuple-element.232, s32[4,12]{1,0:T(4,128)S(1)} %dynamic-slice_bitcast_fusion.2), kind=kOutput, calls=%fused_computation.1.clone.1 | convolution fusion | flops 204473856 | bytes 10485952 | tf_op jit(solution)/shard_map/while/body/eval_jaxpr/while/body/eval_jaxpr/qkn,njhc->qkjhc/dot_general | solution.py:47
  299.9 15.0 %fusion.57 = f32[4,128,4,128]{1,3,2,0:T(8,128)S(1)} fusion(bf16[4,12,128,4,128]{4,1,3,2,0:T(8,128)(2,1)} %convolution_convert_fusion.4, bf16[4,12,128,4,128]{4,1,3,2,0:T(8,128)(2,1)} %convolution_convert_fusion.5, bf16[8,4,128,4,128]{4,2,1,0,3:T(8,128)(2,1)} %get-tuple-element.231, s32[]{:T(128)} %get-tuple-element.218), kind=kOutput, calls=%fused_computation.10.clone.1 | convolution fusion | flops 1613758464 | bytes 18350592 | tf_op jit(solution)/shard_map/while/body/eval_jaxpr/while/body/eval_jaxpr/qhbkj,qkjhd->qbhd/dot_general | solution.py:56
  317.7 8.0 %convolution_convert_fusion.4 = bf16[4,12,128,4,128]{4,1,3,2,0:T(8,128)(2,1)} fusion(bf16[32,128,4,128]{3,0,2,1:T(8,128)(2,1)} %get-tuple-element.232, s32[4,12]{1,0:T(4,128)S(1)} %dynamic-slice_bitcast_fusion.2), kind=kOutput, calls=%fused_computation.1.clone.1 | convolution fusion | flops 204473856 | bytes 10485952 | tf_op jit(solution)/shard_map/while/body/eval_jaxpr/while/body/eval_jaxpr/qkn,njhc->qkjhc/dot_general | solution.py:47
  331.4 15.0 %fusion.57 = f32[4,128,4,128]{1,3,2,0:T(8,128)S(1)} fusion(bf16[4,12,128,4,128]{4,1,3,2,0:T(8,128)(2,1)} %convolution_convert_fusion.4, bf16[4,12,128,4,128]{4,1,3,2,0:T(8,128)(2,1)} %convolution_convert_fusion.5, bf16[8,4,128,4,128]{4,2,1,0,3:T(8,128)(2,1)} %get-tuple-element.231, s32[]{:T(128)} %get-tuple-element.218), kind=kOutput, calls=%fused_computation.10.clone.1 | convolution fusion | flops 1613758464 | bytes 18350592 | tf_op jit(solution)/shard_map/while/body/eval_jaxpr/while/body/eval_jaxpr/qhbkj,qkjhd->qbhd/dot_general | solution.py:56
  349.2 8.0 %convolution_convert_fusion.4 = bf16[4,12,128,4,128]{4,1,3,2,0:T(8,128)(2,1)} fusion(bf16[32,128,4,128]{3,0,2,1:T(8,128)(2,1)} %get-tuple-element.232, s32[4,12]{1,0:T(4,128)S(1)} %dynamic-slice_bitcast_fusion.2), kind=kOutput, calls=%fused_computation.1.clone.1 | convolution fusion | flops 204473856 | bytes 10485952 | tf_op jit(solution)/shard_map/while/body/eval_jaxpr/while/body/eval_jaxpr/qkn,njhc->qkjhc/dot_general | solution.py:47
  362.9 15.0 %fusion.57 = f32[4,128,4,128]{1,3,2,0:T(8,128)S(1)} fusion(bf16[4,12,128,4,128]{4,1,3,2,0:T(8,128)(2,1)} %convolution_convert_fusion.4, bf16[4,12,128,4,128]{4,1,3,2,0:T(8,128)(2,1)} %convolution_convert_fusion.5, bf16[8,4,128,4,128]{4,2,1,0,3:T(8,128)(2,1)} %get-tuple-element.231, s32[]{:T(128)} %get-tuple-element.218), kind=kOutput, calls=%fused_computation.10.clone.1 | convolution fusion | flops 1613758464 | bytes 18350592 | tf_op jit(solution)/shard_map/while/body/eval_jaxpr/while/body/eval_jaxpr/qhbkj,qkjhd->qbhd/dot_general | solution.py:56
  380.7 8.0 %convolution_convert_fusion.4 = bf16[4,12,128,4,128]{4,1,3,2,0:T(8,128)(2,1)} fusion(bf16[32,128,4,128]{3,0,2,1:T(8,128)(2,1)} %get-tuple-element.232, s32[4,12]{1,0:T(4,128)S(1)} %dynamic-slice_bitcast_fusion.2), kind=kOutput, calls=%fused_computation.1.clone.1 | convolution fusion | flops 204473856 | bytes 10485952 | tf_op jit(solution)/shard_map/while/body/eval_jaxpr/while/body/eval_jaxpr/qkn,njhc->qkjhc/dot_general | solution.py:47
  394.4 15.0 %fusion.57 = f32[4,128,4,128]{1,3,2,0:T(8,128)S(1)} fusion(bf16[4,12,128,4,128]{4,1,3,2,0:T(8,128)(2,1)} %convolution_convert_fusion.4, bf16[4,12,128,4,128]{4,1,3,2,0:T(8,128)(2,1)} %convolution_convert_fusion.5, bf16[8,4,128,4,128]{4,2,1,0,3:T(8,128)(2,1)} %get-tuple-element.231, s32[]{:T(128)} %get-tuple-element.218), kind=kOutput, calls=%fused_computation.10.clone.1 | convolution fusion | flops 1613758464 | bytes 18350592 | tf_op jit(solution)/shard_map/while/body/eval_jaxpr/while/body/eval_jaxpr/qhbkj,qkjhd->qbhd/dot_general | solution.py:56
  412.2 8.0 %convolution_convert_fusion.4 = bf16[4,12,128,4,128]{4,1,3,2,0:T(8,128)(2,1)} fusion(bf16[32,128,4,128]{3,0,2,1:T(8,128)(2,1)} %get-tuple-element.232, s32[4,12]{1,0:T(4,128)S(1)} %dynamic-slice_bitcast_fusion.2), kind=kOutput, calls=%fused_computation.1.clone.1 | convolution fusion | flops 204473856 | bytes 10485952 | tf_op jit(solution)/shard_map/while/body/eval_jaxpr/while/body/eval_jaxpr/qkn,njhc->qkjhc/dot_general | solution.py:47
  425.9 15.0 %fusion.57 = f32[4,128,4,128]{1,3,2,0:T(8,128)S(1)} fusion(bf16[4,12,128,4,128]{4,1,3,2,0:T(8,128)(2,1)} %convolution_convert_fusion.4, bf16[4,12,128,4,128]{4,1,3,2,0:T(8,128)(2,1)} %convolution_convert_fusion.5, bf16[8,4,128,4,128]{4,2,1,0,3:T(8,128)(2,1)} %get-tuple-element.231, s32[]{:T(128)} %get-tuple-element.218), kind=kOutput, calls=%fused_computation.10.clone.1 | convolution fusion | flops 1613758464 | bytes 18350592 | tf_op jit(solution)/shard_map/while/body/eval_jaxpr/while/body/eval_jaxpr/qhbkj,qkjhd->qbhd/dot_general | solution.py:56
  449.5 50.7 %all_to_all.60 = bf16[1,4096,4,128]{3,2,0,1:T(4,128)(2,1)S(1)} all-to-all(bf16[1,4096,4,128]{3,2,0,1:T(4,128)(2,1)S(1)} %copy.99), channel_id=1, replica_groups=mesh['groups'=2,'tm'=4,'tok'=4] {'tok'}, dimensions={1} | all-to-all | bytes 8388608 | tf_op jit(solution)/shard_map/all_to_all | solution.py:70
  509.1 14.0 %convert_bitcast_fusion = bf16[1,1024,2048]{2,1,0:T(8,128)(2,1)} fusion(bf16[1024,2048]{0,1:T(8,128)(2,1)} %bitcast.114, bf16[2048,2048]{1,0:T(8,128)(2,1)} %all-gather.4.cloned.1.call-done), kind=kOutput, calls=%fused_computation.29 | convolution fusion | flops 8592031744 | bytes 16777216 | tf_op jit(solution)/shard_map/ftc,cd->ftd/dot_general | solution.py:72
  (112 shorter events, 162.3 us)
Async XLA Ops:
  13.0 52.5 %all-to-all-start.2 = ((bf16[1,1024,16,128]{1,3,0,2:T(8,128)(2,1)}), bf16[1,1024,16,128]{1,3,0,2:T(8,128)(2,1)}, u32[]{:S(2)}, u32[]{:S(2)}) async-start(bf16[1,1024,16,128]{1,3,0,2:T(8,128)(2,1)} %bitcast.107), calls=%async_computation.2 | async-start | bytes 8388608 | tf_op jit(solution)/shard_map/all_to_all | solution.py:20
  65.5 53.5 %all-to-all-start = ((bf16[1,1024,16,128]{1,3,0,2:T(8,128)(2,1)}), bf16[1,1024,16,128]{1,3,0,2:T(8,128)(2,1)}, u32[]{:S(2)}, u32[]{:S(2)}) async-start(bf16[1,1024,16,128]{1,3,0,2:T(8,128)(2,1)} %bitcast.106), calls=%async_computation | async-start | bytes 8388608 | tf_op jit(solution)/shard_map/all_to_all | solution.py:21
  119.0 54.1 %all-to-all-start.1 = ((bf16[1,1024,16,128]{1,3,0,2:T(8,128)(2,1)}), bf16[1,1024,16,128]{1,3,0,2:T(8,128)(2,1)}, u32[]{:S(2)}, u32[]{:S(2)}) async-start(bf16[1,1024,16,128]{1,3,0,2:T(8,128)(2,1)} %bitcast.105), calls=%async_computation.1 | async-start | bytes 8388608 | tf_op jit(solution)/shard_map/all_to_all | solution.py:19
  124.7 64.7 %all-gather.6.cloned.1.call-start = ((), (), s32[]{:S(2)}) async-start(), calls=%async_computation.5 | async-start | bytes 1310720 | tf_op jit(solution)/shard_map/all_gather | solution.py:27
  152.9 4.6 copy-start.3
  155.6 1.9 copy-start.1
  157.5 2.8 copy-start.4
  157.5 2.9 copy-start.5
  159.5 349.6 %all-gather.4.cloned.1.call-start = ((), (), s32[]{:S(2)}) async-start(), calls=%async_computation.4 | async-start | bytes 10485760 | tf_op jit(solution)/shard_map/all_gather | solution.py:75
  160.4 3.5 copy-start.2
  190.9 8.7 %copy-start = (bf16[32,128,4,128]{3,0,2,1:T(8,128)(2,1)S(1)}, bf16[32,128,4,128]{3,0,2,1:T(8,128)(2,1)}, u32[]{:S(2)}) copy-start(bf16[32,128,4,128]{3,0,2,1:T(8,128)(2,1)} %get-tuple-element.230) | copy-start | bytes 12582916 | tf_op jit(solution)/shard_map/while/body/eval_jaxpr/while
  223.1 8.0 %copy-start = (bf16[32,128,4,128]{3,0,2,1:T(8,128)(2,1)S(1)}, bf16[32,128,4,128]{3,0,2,1:T(8,128)(2,1)}, u32[]{:S(2)}) copy-start(bf16[32,128,4,128]{3,0,2,1:T(8,128)(2,1)} %get-tuple-element.230) | copy-start | bytes 12582916 | tf_op jit(solution)/shard_map/while/body/eval_jaxpr/while
  254.6 8.0 %copy-start = (bf16[32,128,4,128]{3,0,2,1:T(8,128)(2,1)S(1)}, bf16[32,128,4,128]{3,0,2,1:T(8,128)(2,1)}, u32[]{:S(2)}) copy-start(bf16[32,128,4,128]{3,0,2,1:T(8,128)(2,1)} %get-tuple-element.230) | copy-start | bytes 12582916 | tf_op jit(solution)/shard_map/while/body/eval_jaxpr/while
  286.2 8.0 %copy-start = (bf16[32,128,4,128]{3,0,2,1:T(8,128)(2,1)S(1)}, bf16[32,128,4,128]{3,0,2,1:T(8,128)(2,1)}, u32[]{:S(2)}) copy-start(bf16[32,128,4,128]{3,0,2,1:T(8,128)(2,1)} %get-tuple-element.230) | copy-start | bytes 12582916 | tf_op jit(solution)/shard_map/while/body/eval_jaxpr/while
  317.7 8.0 %copy-start = (bf16[32,128,4,128]{3,0,2,1:T(8,128)(2,1)S(1)}, bf16[32,128,4,128]{3,0,2,1:T(8,128)(2,1)}, u32[]{:S(2)}) copy-start(bf16[32,128,4,128]{3,0,2,1:T(8,128)(2,1)} %get-tuple-element.230) | copy-start | bytes 12582916 | tf_op jit(solution)/shard_map/while/body/eval_jaxpr/while
  349.2 8.0 %copy-start = (bf16[32,128,4,128]{3,0,2,1:T(8,128)(2,1)S(1)}, bf16[32,128,4,128]{3,0,2,1:T(8,128)(2,1)}, u32[]{:S(2)}) copy-start(bf16[32,128,4,128]{3,0,2,1:T(8,128)(2,1)} %get-tuple-element.230) | copy-start | bytes 12582916 | tf_op jit(solution)/shard_map/while/body/eval_jaxpr/while
  380.7 8.0 %copy-start = (bf16[32,128,4,128]{3,0,2,1:T(8,128)(2,1)S(1)}, bf16[32,128,4,128]{3,0,2,1:T(8,128)(2,1)}, u32[]{:S(2)}) copy-start(bf16[32,128,4,128]{3,0,2,1:T(8,128)(2,1)} %get-tuple-element.230) | copy-start | bytes 12582916 | tf_op jit(solution)/shard_map/while/body/eval_jaxpr/while
  412.2 8.0 %copy-start = (bf16[32,128,4,128]{3,0,2,1:T(8,128)(2,1)S(1)}, bf16[32,128,4,128]{3,0,2,1:T(8,128)(2,1)}, u32[]{:S(2)}) copy-start(bf16[32,128,4,128]{3,0,2,1:T(8,128)(2,1)} %get-tuple-element.230) | copy-start | bytes 12582916 | tf_op jit(solution)/shard_map/while/body/eval_jaxpr/while
Sparse Core Ops, SparseCore 0:
  159.6 29.7 all-gather.5
  190.9 58.3 all-gather.3
where the time goes:
time: 533 us; the launch traced here: 530 us
  matrix products  258 us (48%)
  local copies, waits for them, and re-layouts  100 us (19%)
  waiting for transfers between devices  88.3 us (17%)
  blocking collectives  50.7 us (10%)
  starting transfers between devices  16.7 us (3%)
  between operations  13.5 us (3%)
    dot_general x8, matrix products, attend(): jnp.einsum('qhbkj,qkjhd->qbhd', weight, v_sel, preferred_element_type=jnp...  120 us
    dot_general x8, matrix products, attend(): jnp.einsum('qkn,njhc->qkjhc', selector, k_frame, preferred_element_type=j...  64.5 us
    all_to_all x1, blocking collectives, on_device(): lax.all_to_all(attended, 'tok', split_axis=1, concat_axis=2, tiled=True)  50.7 us
    dot_general x8, matrix products, attend(): jnp.einsum('qkn,njhc->qkjhc', selector, v_frame, preferred_element_type=j...  45.7 us
    all_to_all x1, waiting for transfers between devices, on_device(): lax.all_to_all(split_heads(keys), 'tok', split_axis=2, concat_axis=1, til...  41.3 us
    all_to_all x1, waiting for transfers between devices, on_device(): lax.all_to_all(split_heads(values), 'tok', split_axis=2, concat_axis=1, t...  41 us
    unnamed x17, local copies, waits for them, and re-layouts  31.5 us
    all_to_all x3, local copies, waits for them, and re-layouts, on_device(): lax.all_to_all(split_heads(keys), 'tok', split_axis=2, concat_axis=1, til...  16.8 us
  transfers between devices with their start and end apart: 5, of which 3 were waited for; matrix products, arithmetic and copies ran while one was open for 64% of the time, Pallas kernels for 0%

commit v1 on v0

v1 whole, which is shorter than its diff:
```python
import functools

import jax
import jax.numpy as jnp
from jax import lax
from jax.experimental import pallas as pl
from jax.experimental.pallas import tpu as pltpu
from jax.sharding import PartitionSpec as P

HEAD_DIM = 128
BLK = 128
GROUP_HEADS = 2
MESH = pl.DeviceIdType.MESH


def mix_kernel(
    n_tok, n_tm, groups, kblk,
    index_ref, gain_in, q_hbm, k_hbm, v_hbm, out_hbm, *scratch,
):
    states = scratch[:groups]
    (
        kbuf, vbuf, qbuf, att, gain, state_out, state_in, carried,
        in_sem, gain_local, gain_send, gain_recv, far_send, far_recv, near_send, near_recv,
        fwd_send, fwd_recv, st_send, st_recv, out_sem,
    ) = scratch[groups:]
    rows = kbuf.shape[0]
    per_dev = rows // BLK
    heads_dev = gain.shape[2] // HEAD_DIM
    width = GROUP_HEADS * HEAD_DIM
    chips = n_tok // 2
    tok = lax.axis_index("tok")
    tm = lax.axis_index("tm")
    chip, core = tok // 2, tok % 2
    sibling = chip * 2 + (1 - core)

    def far(step):
        return lax.rem(chip + step, chips) * 2 + core

    def far_source(step):
        return lax.rem(chip + chips - step, chips) * 2 + core

    barrier = pltpu.get_barrier_semaphore()
    for step in range(1, n_tok):
        pl.semaphore_signal(
            barrier, inc=1, device_id={"tok": lax.rem(tok + step, n_tok)}, device_id_type=MESH
        )
    for step in range(1, n_tm):
        pl.semaphore_signal(
            barrier, inc=1, device_id={"tm": lax.rem(tm + step, n_tm)}, device_id_type=MESH
        )

    def load(g, which):
        source, target = ((k_hbm, kbuf), (v_hbm, vbuf), (q_hbm, qbuf))[which]
        cols = pl.ds(g * width, width)
        return pltpu.make_async_copy(
            source.at[0, :, cols], target.at[:, cols], in_sem.at[which, g]
        )

    for g in range(groups):
        load(g, 0).start()
        load(g, 1).start()
    for g in range(groups):
        load(g, 2).start()
    own_gain = pltpu.make_async_copy(gain_in, gain.at[tok], gain_local)
    own_gain.start()
    pl.semaphore_wait(barrier, n_tok - 1 + n_tm - 1)

    def gain_copy(step, source):
        return pltpu.make_async_remote_copy(
            src_ref=gain_in, dst_ref=gain.at[source], send_sem=gain_send.at[step],
            recv_sem=gain_recv.at[step], device_id={"tok": lax.rem(tok + step, n_tok)},
            device_id_type=MESH,
        )

    for step in range(1, n_tok):
        gain_copy(step, tok).start()

    def piece(g, owner):
        return states[g].at[pl.ds(owner * per_dev, per_dev)]

    def far_copy(g, step, owner):
        return pltpu.make_async_remote_copy(
            src_ref=piece(g, owner), dst_ref=piece(g, owner), send_sem=far_send.at[g, step],
            recv_sem=far_recv.at[g, step], device_id={"tok": far(step)}, device_id_type=MESH,
        )

    def near_copy(g, owner):
        return pltpu.make_async_remote_copy(
            src_ref=piece(g, owner), dst_ref=piece(g, owner), send_sem=near_send.at[g],
            recv_sem=near_recv.at[g], device_id={"tok": sibling}, device_id_type=MESH,
        )

    def forward_copy(g, step, owner):
        return pltpu.make_async_remote_copy(
            src_ref=piece(g, owner), dst_ref=piece(g, owner), send_sem=fwd_send.at[g, step],
            recv_sem=fwd_recv.at[g, step], device_id={"tok": sibling}, device_id_type=MESH,
        )

    def state_copy(g, step):
        return pltpu.make_async_remote_copy(
            src_ref=state_out.at[g], dst_ref=state_in.at[g, step], send_sem=st_send.at[g, step],
            recv_sem=st_recv.at[g, step], device_id={"tm": lax.rem(tm + step, n_tm)},
            device_id_type=MESH,
        )

    for g in range(groups):
        load(g, 0).wait()
        load(g, 1).wait()

        def block_state(j, _, g=g):
            at = pl.ds(pl.multiple_of(j * BLK, BLK), BLK)
            for h in range(GROUP_HEADS):
                cols = pl.ds(g * width + h * HEAD_DIM, HEAD_DIM)
                product = lax.dot_general(
                    kbuf[at, cols], vbuf[at, cols], (((0,), (0,)), ((), ())),
                    preferred_element_type=jnp.float32,
                )
                states[g][tok * per_dev + j, h] = product.astype(jnp.bfloat16)
            return 0

        lax.fori_loop(0, per_dev, block_state, 0)
        for step in range(1, chips):
            far_copy(g, step, tok).start()
        near_copy(g, tok).start()

    own_gain.wait()
    for step in range(1, n_tok):
        gain_copy(step, lax.rem(tok + n_tok - step, n_tok)).wait_recv()

    def arrive(g):
        for step in range(1, chips):
            far_copy(g, step, far_source(step)).wait_recv()
            forward_copy(g, step, far_source(step)).start()

    def frame_state(g):
        near_copy(g, sibling).wait_recv()
        for step in range(1, chips):
            source = lax.rem(chip + chips - step, chips) * 2 + (1 - core)
            forward_copy(g, step, source).wait_recv()
        for h in range(GROUP_HEADS):
            def add(n, total, h=h):
                for u in range(4):
                    total = total + states[g][n * 4 + u, h].astype(jnp.float32)
                return total

            total = lax.fori_loop(
                0, n_tok * per_dev // 4, add, jnp.zeros((HEAD_DIM, HEAD_DIM), jnp.float32)
            )
            state_out[g, h] = total.astype(jnp.bfloat16)
        for step in range(1, n_tm):
            state_copy(g, step).start()

    def attend(g):
        load(g, 2).wait()
        for step in range(1, n_tm):
            state_copy(g, step).wait_recv()
        for h in range(GROUP_HEADS):
            total = jnp.zeros((HEAD_DIM, HEAD_DIM), jnp.float32)
            for step in range(1, n_tm):
                earlier = (tm >= step).astype(jnp.float32)
                total = total + state_in[g, step, h].astype(jnp.float32) * earlier
            carried[h] = total

        def block(b, _):
            at = pl.ds(pl.multiple_of(b * BLK, BLK), BLK)
            chosen = [index_ref[0, tok * per_dev + b, i] for i in range(kblk)]
            for h in range(GROUP_HEADS):
                head = g * GROUP_HEADS + h
                cols = pl.ds(head * HEAD_DIM, HEAD_DIM)
                total = carried[h]
                for i in range(kblk):
                    total = total + states[g][chosen[i], h].astype(jnp.float32)
                mixed = jnp.dot(
                    qbuf[at, cols], total.astype(jnp.bfloat16), preferred_element_type=jnp.float32
                )
                scale = lax.rsqrt(jnp.mean(mixed * mixed, axis=-1, keepdims=True) + 1e-06)
                g_row = gain[head // heads_dev, 0:1, pl.ds((head % heads_dev) * HEAD_DIM, HEAD_DIM)]
                att[at, cols] = (mixed * scale * g_row).astype(jnp.bfloat16)
            return 0

        lax.fori_loop(0, per_dev, block, 0)
        store(g).start()

    def store(g):
        cols = pl.ds(g * width, width)
        return pltpu.make_async_copy(att.at[:, cols], out_hbm.at[:, cols], out_sem.at[g])

    for turn in range(groups + 2):
        if turn < groups:
            arrive(turn)
        if 0 <= turn - 1 < groups:
            frame_state(turn - 1)
        if 0 <= turn - 2 < groups:
            attend(turn - 2)

    for g in range(groups):
        store(g).wait()
        near_copy(g, tok).wait_send()
        for step in range(1, chips):
            far_copy(g, step, tok).wait_send()
            forward_copy(g, step, far_source(step)).wait_send()
        for step in range(1, n_tm):
            state_copy(g, step).wait_send()
    for step in range(1, n_tok):
        gain_copy(step, tok).wait_send()


def on_device(n_tok, n_tm, queries, keys, values, block_index, norm_gain, out_weight):
    rows, model_width = queries.shape[1:]
    kblk = block_index.shape[2]
    heads = model_width // HEAD_DIM
    groups = heads // GROUP_HEADS
    chips = n_tok // 2
    blocks = n_tok * rows // BLK
    gain_rows = jnp.broadcast_to(norm_gain.astype(jnp.float32)[None], (8, norm_gain.shape[0]))
    weight = lax.all_gather(out_weight, "tok", axis=0, tiled=True)
    dma = pltpu.SemaphoreType.DMA
    attended = pl.pallas_call(
        functools.partial(mix_kernel, n_tok, n_tm, groups, kblk),
        out_shape=jax.ShapeDtypeStruct((rows, model_width), jnp.bfloat16),
        in_specs=[
            pl.BlockSpec(memory_space=pltpu.SMEM),
            pl.BlockSpec(memory_space=pltpu.VMEM),
            pl.BlockSpec(memory_space=pl.ANY),
            pl.BlockSpec(memory_space=pl.ANY),
            pl.BlockSpec(memory_space=pl.ANY),
        ],
        out_specs=pl.BlockSpec(memory_space=pl.ANY),
        scratch_shapes=[
            pltpu.VMEM((blocks, GROUP_HEADS, HEAD_DIM, HEAD_DIM), jnp.bfloat16)
            for _ in range(groups)
        ] + [
            pltpu.VMEM((rows, model_width), jnp.bfloat16),
            pltpu.VMEM((rows, model_width), jnp.bfloat16),
            pltpu.VMEM((rows, model_width), jnp.bfloat16),
            pltpu.VMEM((rows, model_width), jnp.bfloat16),
            pltpu.VMEM((n_tok,) + gain_rows.shape, jnp.float32),
            pltpu.VMEM((groups, GROUP_HEADS, HEAD_DIM, HEAD_DIM), jnp.bfloat16),
            pltpu.VMEM((groups, n_tm, GROUP_HEADS, HEAD_DIM, HEAD_DIM), jnp.bfloat16),
            pltpu.VMEM((GROUP_HEADS, HEAD_DIM, HEAD_DIM), jnp.float32),
            dma((3, groups)),
            dma(()),
            dma((n_tok,)),
            dma((n_tok,)),
            dma((groups, chips)),
            dma((groups, chips)),
            dma((groups,)),
            dma((groups,)),
            dma((groups, chips)),
            dma((groups, chips)),
            dma((groups, n_tm)),
            dma((groups, n_tm)),
            dma((groups,)),
        ],
        compiler_params=pltpu.CompilerParams(
            collective_id=0, has_side_effects=True, vmem_limit_bytes=56 * 1024 * 1024
        ),
        cost_estimate=pl.CostEstimate(
            flops=8 * rows * model_width * HEAD_DIM, bytes_accessed=400_000_000, transcendentals=0
        ),
    )(block_index, gain_rows, queries, keys, values)
    total = jnp.dot(attended, weight, preferred_element_type=jnp.float32)
    return total.astype(jnp.bfloat16)[None]


def solution(mesh):
    in_specs = (
        P(("groups", "tm"), "tok", None),
        P(("groups", "tm"), "tok", None),
        P(("groups", "tm"), "tok", None),
        P(("groups", "tm"), None, None),
        P("tok"),
        P("tok", None),
    )
    out_specs = P(("groups", "tm"), "tok", None)
    return jax.shard_map(
        functools.partial(on_device, mesh.shape["tok"], mesh.shape["tm"]),
        mesh=mesh, in_specs=in_specs, out_specs=out_specs, check_vma=False,
    )
```

time: 533 us -> 192 us (0.36)
  matrix products: 258 us -> 13.8 us
  Pallas kernels: 0 us -> 158 us
  local copies, waits for them, and re-layouts: 100 us -> 2.65 us
  waiting for transfers between devices: 88.3 us -> 0.73 us
  blocking collectives: 50.7 us -> 0 us
  starting transfers between devices: 16.7 us -> 0.01 us
    dot_general x34 -> x1, matrix products: 258 us -> 13.8 us  [on_device(): total = jnp.dot(attended, weight, preferred_element_type=jnp.float32)]
    pallas_call x0 -> x1, Pallas kernels: none -> 158 us  [on_device(): pl.pallas_call(functools.partial(mix_kernel, n_tok, n_tm, groups, kblk),...]
    all_to_all x3 -> x0, waiting for transfers between devices: 82.3 us -> none  [the longest x1 41.3 us: on_device(): lax.all_to_all(split_heads(keys), 'tok', split_axis=2, concat_axis=1, til...]
    all_to_all x1 -> x0, blocking collectives: 50.7 us -> none  [on_device(): lax.all_to_all(attended, 'tok', split_axis=1, concat_axis=2, tiled=True)]
    all_to_all x9 -> x0, local copies, waits for them, and re-layouts: 45.6 us -> none  [the longest x3 16.8 us: on_device(): lax.all_to_all(split_heads(keys), 'tok', split_axis=2, concat_axis=1, til...]
    unnamed x17 -> x1, local copies, waits for them, and re-layouts: 31.5 us -> 1.38 us
    all_to_all x3 -> x0, starting transfers between devices: 16.6 us -> none  [the longest x1 6.1 us: on_device(): lax.all_to_all(split_heads(values), 'tok', split_axis=2, concat_axis=1, t...]
    dynamic_update_slice x16 -> x0, local copies, waits for them, and re-layouts: 9.37 us -> none  [per_frame(): return lax.map(attend, (q_frame, index_frame))]
  transfers between devices with their start and end apart: 5 -> 1, of which waited for: 3 -> 0; matrix products, arithmetic and copies ran while one was open for 64% -> 1% of each run, Pallas kernels for 0% -> 84%
where the time goes in v1:
time: 192 us; the launch traced here: 189 us
  Pallas kernels  158 us (82%)
  matrix products  13.8 us (7%)
  between operations  13.4 us (7%)
  local copies, waits for them, and re-layouts  2.65 us (1%)
    pallas_call x1, Pallas kernels, on_device(): pl.pallas_call(functools.partial(mix_kernel, n_tok, n_tm, groups, kblk),...  158 us
    dot_general x1, matrix products, on_device(): total = jnp.dot(attended, weight, preferred_element_type=jnp.float32)  13.8 us
  transfers between devices with their start and end apart: 1, of which 0 were waited for; matrix products, arithmetic and copies ran while one was open for 1% of the time, Pallas kernels for 84%

profile of v1, /device:TPU:1, one launch (start us, length us, event | category | flops | bytes accessed | tf_op | source)
XLA Modules:
  0.0 188.5 jit_solution(11423748552777167500)
XLA Ops:
  6.5 0.0 all-gather.2.cloned.1.call-start
  6.5 0.7 all-gather.2.cloned.1.call-update
  7.3 1.4 copy.7.index_ref
  8.6 1.3 broadcast_in_dim.4.gain_in
  9.9 157.9 %shard_map.64 = bf16[1024,2048]{1,0:T(8,128)(2,1)} custom-call(s32[1,32,12]{2,1,0:T(8,128)} %copy.7.index_ref, f32[8,512]{1,0:T(8,128)} %broadcast_in_dim.4.gain_in, bf16[1,1024,2048]{2,1,0:T(8,128)(2,1)} %q_hbm.1, bf16[1,1024,2048]{2,1,0:T(8,128)(2,1)} %k_hbm.1, bf16[1,1024,2048]{2,1,0:T(8,128)(2,1)} %v_hbm.1), custom_call_target="tpu_custom_call" | custom-call | flops 2147483648 | bytes 400000000 | tf_op jit(solution)/shard_map/pallas_call | solution.py:218
  167.9 0.0 all-gather.2.cloned.1.call-done
  167.9 13.8 %convert_bitcast_fusion = bf16[1,1024,2048]{2,1,0:T(8,128)(2,1)} fusion(bf16[1024,2048]{1,0:T(8,128)(2,1)} %shard_map.64, bf16[2048,2048]{1,0:T(8,128)(2,1)} %all-gather.2.cloned.1.call-done), kind=kOutput, calls=%fused_computation | convolution fusion | flops 8592031744 | bytes 16777216 | tf_op jit(solution)/shard_map/dot_general | solution.py:262
Async XLA Ops:
  6.5 161.4 %all-gather.2.cloned.1.call-start = ((), (), s32[]{:S(2)}) async-start(), calls=%async_computation | async-start | bytes 10485760 | tf_op jit(solution)/shard_map/all_gather | solution.py:216
Sparse Core Ops, SparseCore 0:
  8.9 105.9 all-gather.1

commit v2 on v1

--- a/solution.py
+++ b/solution.py
@@ -14,14 +14,15 @@
 
 
 def mix_kernel(
-    n_tok, n_tm, groups, kblk,
-    index_ref, gain_in, q_hbm, k_hbm, v_hbm, out_hbm, *scratch,
+    n_tok, n_tm, columns, groups, kblk,
+    index_ref, gain_in, q_hbm, k_hbm, v_hbm, w_hbm, out_hbm, *scratch,
 ):
     states = scratch[:groups]
     (
-        kbuf, vbuf, qbuf, att, gain, state_out, state_in, carried,
+        kbuf, vbuf, qbuf, att, weight, acc, gain, state_out, state_in, carried,
         in_sem, gain_local, gain_send, gain_recv, far_send, far_recv, near_send, near_recv,
         fwd_send, fwd_recv, st_send, st_recv, out_sem,
+        w_local, ws_send, ws_recv, wf_send, wf_recv, wb_send, wb_recv, wn_send, wn_recv,
     ) = scratch[groups:]
     rows = kbuf.shape[0]
     per_dev = rows // BLK
@@ -32,6 +33,17 @@
     tm = lax.axis_index("tm")
     chip, core = tok // 2, tok % 2
     sibling = chip * 2 + (1 - core)
+    column = lax.axis_index("groups") * n_tm + tm
+    w_rows = w_hbm.shape[0]
+    w_cols = weight.shape[2]
+    tile = min(rows, 256)
+
+    def column_peer(step):
+        peer = lax.rem(column + step, columns)
+        return {"groups": peer // n_tm, "tm": peer % n_tm}
+
+    def column_source(step):
+        return lax.rem(column + columns - step, columns)
 
     def far(step):
         return lax.rem(chip + step, chips) * 2 + core
@@ -44,10 +56,8 @@
         pl.semaphore_signal(
             barrier, inc=1, device_id={"tok": lax.rem(tok + step, n_tok)}, device_id_type=MESH
         )
-    for step in range(1, n_tm):
-        pl.semaphore_signal(
-            barrier, inc=1, device_id={"tm": lax.rem(tm + step, n_tm)}, device_id_type=MESH
-        )
+    for step in range(1, columns):
+        pl.semaphore_signal(barrier, inc=1, device_id=column_peer(step), device_id_type=MESH)
 
     def load(g, which):
         source, target = ((k_hbm, kbuf), (v_hbm, vbuf), (q_hbm, qbuf))[which]
@@ -63,7 +73,46 @@
         load(g, 2).start()
     own_gain = pltpu.make_async_copy(gain_in, gain.at[tok], gain_local)
     own_gain.start()
-    pl.semaphore_wait(barrier, n_tok - 1 + n_tm - 1)
+    pl.semaphore_wait(barrier, n_tok - 1 + columns - 1)
+
+    def w_part(part, owner):
+        return weight.at[part, pl.ds(pl.multiple_of(owner * w_rows, w_rows), w_rows)]
+
+    def w_source(part):
+        return w_hbm.at[:, pl.ds(pl.multiple_of(part * w_cols, w_cols), w_cols)]
+
+    def w_local_copy(part):
+        return pltpu.make_async_copy(w_source(part), w_part(part, tok), w_local.at[part])
+
+    def w_near_copy(part, owner):
+        return pltpu.make_async_remote_copy(
+            src_ref=w_source(part), dst_ref=w_part(part, owner), send_sem=ws_send.at[part],
+            recv_sem=ws_recv.at[part], device_id={"tok": sibling}, device_id_type=MESH,
+        )
+
+    def w_far_copy(step, owner):
+        return pltpu.make_async_remote_copy(
+            src_ref=w_source(column), dst_ref=w_part(column, owner), send_sem=wf_send.at[step],
+            recv_sem=wf_recv.at[step], device_id={"tok": far(step)}, device_id_type=MESH,
+        )
+
+    def w_spread_copy(step, hop, part):
+        return pltpu.make_async_remote_copy(
+            src_ref=w_part(part, far_source(step)), dst_ref=w_part(part, far_source(step)),
+            send_sem=wb_send.at[step, hop], recv_sem=wb_recv.at[step, hop],
+            device_id=column_peer(hop), device_id_type=MESH,
+        )
+
+    def w_forward_copy(step, hop, owner):
+        part = column_source(hop)
+        return pltpu.make_async_remote_copy(
+            src_ref=w_part(part, owner), dst_ref=w_part(part, owner),
+            send_sem=wn_send.at[step, hop], recv_sem=wn_recv.at[step, hop],
+            device_id={"tok": sibling}, device_id_type=MESH,
+        )
+
+    for step in range(1, chips):
+        w_far_copy(step, tok).start()
 
     def gain_copy(step, source):
         return pltpu.make_async_remote_copy(
@@ -123,6 +172,14 @@
             far_copy(g, step, tok).start()
         near_copy(g, tok).start()
 
+    for step in range(1, chips):
+        w_far_copy(step, far_source(step)).wait_recv()
+        for hop in range(1, columns):
+            w_spread_copy(step, hop, column).start()
+    for part in range(columns):
+        w_local_copy(part).start()
+        w_near_copy(part, tok).start()
+
     own_gain.wait()
     for step in range(1, n_tok):
         gain_copy(step, lax.rem(tok + n_tok - step, n_tok)).wait_recv()
@@ -170,8 +227,13 @@
                 total = carried[h]
                 for i in range(kblk):
                     total = total + states[g][chosen[i], h].astype(jnp.float32)
+                high = total.astype(jnp.bfloat16)
+                low = (total - high.astype(jnp.float32)).astype(jnp.bfloat16)
+                q_block = qbuf[at, cols]
                 mixed = jnp.dot(
-                    qbuf[at, cols], total.astype(jnp.bfloat16), preferred_element_type=jnp.float32
+                    jnp.concatenate([q_block, q_block], axis=1),
+                    jnp.concatenate([high, low], axis=0),
+                    preferred_element_type=jnp.float32,
                 )
                 scale = lax.rsqrt(jnp.mean(mixed * mixed, axis=-1, keepdims=True) + 1e-06)
                 g_row = gain[head // heads_dev, 0:1, pl.ds((head % heads_dev) * HEAD_DIM, HEAD_DIM)]
@@ -179,22 +241,80 @@
             return 0
 
         lax.fori_loop(0, per_dev, block, 0)
-        store(g).start()
-
-    def store(g):
-        cols = pl.ds(g * width, width)
-        return pltpu.make_async_copy(att.at[:, cols], out_hbm.at[:, cols], out_sem.at[g])
-
+
+    def forward_weight():
+        for step in range(1, chips):
+            for hop in range(columns):
+                if hop:
+                    w_spread_copy(step, hop, column_source(hop)).wait_recv()
+                w_forward_copy(step, hop, far_source(step)).start()
+
+    def await_weight():
+        for part in range(columns):
+            w_local_copy(part).wait()
+            w_near_copy(part, sibling).wait_recv()
+        for step in range(1, chips):
+            for hop in range(columns):
+                source = lax.rem(chip + chips - step, chips) * 2 + (1 - core)
+                w_forward_copy(step, hop, source).wait_recv()
+
+    def store(r):
+        at = pl.ds(pl.multiple_of(r * tile, tile), tile)
+        return pltpu.make_async_copy(kbuf.at[at], out_hbm.at[0, at], out_sem.at[r])
+
+    def project(low, high, first=False, last=False):
+        depth = pl.ds(low * width, (high - low) * width)
+
+        def row_tile(r, _):
+            at = pl.ds(pl.multiple_of(r * tile, tile), tile)
+
+            def part_of(part, _):
+                cols = pl.ds(pl.multiple_of(part * w_cols, w_cols), w_cols)
+                total = jnp.dot(
+                    att[at, depth], weight[part, depth, :], preferred_element_type=jnp.float32
+                )
+                if not first:
+                    total = total + acc[at, cols]
+                if last:
+                    kbuf[at, cols] = total.astype(jnp.bfloat16)
+                else:
+                    acc[at, cols] = total
+                return 0
+
+            lax.fori_loop(0, columns, part_of, 0)
+            if last:
+                store(r).start()
+            return 0
+
+        lax.fori_loop(0, rows // tile, row_tile, 0)
+
+    half = groups // 2
     for turn in range(groups + 2):
-        if turn < groups:
-            arrive(turn)
         if 0 <= turn - 1 < groups:
             frame_state(turn - 1)
         if 0 <= turn - 2 < groups:
             attend(turn - 2)
-
+        if turn == half:
+            forward_weight()
+        if turn == half + 1:
+            await_weight()
+            project(0, half, first=True)
+        if turn > half + 1:
+            project(turn - 2, turn - 1, last=turn == groups + 1)
+        if turn < groups:
+            arrive(turn)
+
+    for r in range(rows // tile):
+        store(r).wait()
+    for part in range(columns):
+        w_near_copy(part, tok).wait_send()
+    for step in range(1, chips):
+        w_far_copy(step, tok).wait_send()
+        for hop in range(columns):
+            if hop:
+                w_spread_copy(step, hop, column).wait_send()
+            w_forward_copy(step, hop, far_source(step)).wait_send()
     for g in range(groups):
-        store(g).wait()
         near_copy(g, tok).wait_send()
         for step in range(1, chips):
             far_copy(g, step, tok).wait_send()
@@ -205,7 +325,7 @@
         gain_copy(step, tok).wait_send()
 
 
-def on_device(n_tok, n_tm, queries, keys, values, block_index, norm_gain, out_weight):
+def on_device(n_tok, n_tm, columns, queries, keys, values, block_index, norm_gain, out_weight):
     rows, model_width = queries.shape[1:]
     kblk = block_index.shape[2]
     heads = model_width // HEAD_DIM
@@ -213,14 +333,14 @@
     chips = n_tok // 2
     blocks = n_tok * rows // BLK
     gain_rows = jnp.broadcast_to(norm_gain.astype(jnp.float32)[None], (8, norm_gain.shape[0]))
-    weight = lax.all_gather(out_weight, "tok", axis=0, tiled=True)
     dma = pltpu.SemaphoreType.DMA
-    attended = pl.pallas_call(
-        functools.partial(mix_kernel, n_tok, n_tm, groups, kblk),
-        out_shape=jax.ShapeDtypeStruct((rows, model_width), jnp.bfloat16),
+    return pl.pallas_call(
+        functools.partial(mix_kernel, n_tok, n_tm, columns, groups, kblk),
+        out_shape=jax.ShapeDtypeStruct((1, rows, model_width), jnp.bfloat16),
         in_specs=[
             pl.BlockSpec(memory_space=pltpu.SMEM),
             pl.BlockSpec(memory_space=pltpu.VMEM),
+            pl.BlockSpec(memory_space=pl.ANY),
             pl.BlockSpec(memory_space=pl.ANY),
             pl.BlockSpec(memory_space=pl.ANY),
             pl.BlockSpec(memory_space=pl.ANY),
@@ -234,6 +354,8 @@
             pltpu.VMEM((rows, model_width), jnp.bfloat16),
             pltpu.VMEM((rows, model_width), jnp.bfloat16),
             pltpu.VMEM((rows, model_width), jnp.bfloat16),
+            pltpu.VMEM((columns, model_width, model_width // columns), jnp.bfloat16),
+            pltpu.VMEM((rows, model_width), jnp.float32),
             pltpu.VMEM((n_tok,) + gain_rows.shape, jnp.float32),
             pltpu.VMEM((groups, GROUP_HEADS, HEAD_DIM, HEAD_DIM), jnp.bfloat16),
             pltpu.VMEM((groups, n_tm, GROUP_HEADS, HEAD_DIM, HEAD_DIM), jnp.bfloat16),
@@ -250,17 +372,24 @@
             dma((groups, chips)),
             dma((groups, n_tm)),
             dma((groups, n_tm)),
-            dma((groups,)),
+            dma((rows // min(rows, 256),)),
+            dma((columns,)),
+            dma((columns,)),
+            dma((columns,)),
+            dma((chips,)),
+            dma((chips,)),
+            dma((chips, columns)),
+            dma((chips, columns)),
+            dma((chips, columns)),
+            dma((chips, columns)),
         ],
         compiler_params=pltpu.CompilerParams(
-            collective_id=0, has_side_effects=True, vmem_limit_bytes=56 * 1024 * 1024
+            collective_id=0, has_side_effects=True, vmem_limit_bytes=60 * 1024 * 1024
         ),
         cost_estimate=pl.CostEstimate(
             flops=8 * rows * model_width * HEAD_DIM, bytes_accessed=400_000_000, transcendentals=0
         ),
-    )(block_index, gain_rows, queries, keys, values)
-    total = jnp.dot(attended, weight, preferred_element_type=jnp.float32)
-    return total.astype(jnp.bfloat16)[None]
+    )(block_index, gain_rows, queries, keys, values, out_weight)
 
 
 def solution(mesh):
@@ -274,6 +403,6 @@
     )
     out_specs = P(("groups", "tm"), "tok", None)
     return jax.shard_map(
-        functools.partial(on_device, mesh.shape["tok"], mesh.shape["tm"]),
+        functools.partial(on_device, mesh.shape["tok"], mesh.shape["tm"], mesh.shape["groups"] * mesh.shape["tm"]),
         mesh=mesh, in_specs=in_specs, out_specs=out_specs, check_vma=False,
     )

time: 192 us -> 162 us (0.84)
  matrix products: 13.8 us -> 0 us
  between operations: 13.4 us -> 0.01 us
  Pallas kernels: 158 us -> 152 us
  local copies, waits for them, and re-layouts: 2.65 us -> 7.44 us
    dot_general x1 -> x0, matrix products: 13.8 us -> none  [on_device(): total = jnp.dot(attended, weight, preferred_element_type=jnp.float32)]
    pallas_call x1, Pallas kernels: 158 us -> 152 us  [on_device(): pl.pallas_call(functools.partial(mix_kernel, n_tok, n_tm, columns, groups...]
    unnamed x1 -> x2, local copies, waits for them, and re-layouts: 1.38 us -> 6.16 us
  transfers between devices with their start and end apart: 1 -> 0, of which waited for: 0 -> 0; matrix products, arithmetic and copies ran while one was open for 1% -> 0% of each run, Pallas kernels for 84% -> 0%
where the time goes in v2:
time: 162 us; the launch traced here: 159 us
  Pallas kernels  152 us (94%)
  local copies, waits for them, and re-layouts  7.44 us (5%)
    pallas_call x1, Pallas kernels, on_device(): pl.pallas_call(functools.partial(mix_kernel, n_tok, n_tm, columns, groups...  152 us
    unnamed x2, local copies, waits for them, and re-layouts  6.16 us

profile of v2, /device:TPU:1, one launch (start us, length us, event | category | flops | bytes accessed | tf_op | source)
XLA Modules:
  0.0 159.1 jit_solution(15336516586499930202)
XLA Ops:
  0.0 1.4 copy.7.index_ref
  1.4 1.3 broadcast_in_dim.2.gain_in
  2.7 151.7 %shard_map.64 = bf16[1,1024,2048]{2,1,0:T(8,128)(2,1)} custom-call(s32[1,32,12]{2,1,0:T(8,128)} %copy.7.index_ref, f32[8,512]{1,0:T(8,128)} %broadcast_in_dim.2.gain_in, bf16[1,1024,2048]{2,1,0:T(8,128)(2,1)} %q_hbm.1, bf16[1,1024,2048]{2,1,0:T(8,128)(2,1)} %k_hbm.1, bf16[1,1024,2048]{2,1,0:T(8,128)(2,1)} %v_hbm.1, bf16[512,2048]{1,0:T(8,128)(2,1)} %w_hbm.1), custom_call_target="tpu_custom_call" | custom-call | flops 2147483648 | bytes 400000000 | tf_op jit(solution)/shard_map/pallas_call | solution.py:337
  154.4 4.8 %copy.9 = bf16[1,1024,2048]{2,1,0:T(8,128)(2,1)} copy(bf16[1,1024,2048]{2,1,0:T(8,128)(2,1)} %shard_map.64) | data formatting | bytes 8388608

commit v3 on v2

--- a/solution.py
+++ b/solution.py
@@ -33,17 +33,19 @@
     tm = lax.axis_index("tm")
     chip, core = tok // 2, tok % 2
     sibling = chip * 2 + (1 - core)
-    column = lax.axis_index("groups") * n_tm + tm
     w_rows = w_hbm.shape[0]
     w_cols = weight.shape[2]
-    tile = min(rows, 256)
+    scenes = columns // n_tm
+    scene = lax.axis_index("groups")
+    column = scene * n_tm + tm
 
     def column_peer(step):
         peer = lax.rem(column + step, columns)
         return {"groups": peer // n_tm, "tm": peer % n_tm}
 
-    def column_source(step):
-        return lax.rem(column + columns - step, columns)
+    def column_source(hop):
+        section = lax.rem(tm + n_tm - hop % n_tm, n_tm)
+        return lax.rem(scene + scenes - hop // n_tm, scenes) * n_tm + section
 
     def far(step):
         return lax.rem(chip + step, chips) * 2 + core
@@ -97,11 +99,33 @@
         )
 
     def w_spread_copy(step, hop, part):
+        if hop < n_tm:
+            target = {"tm": lax.rem(tm + hop, n_tm)}
+        else:
+            target = {"groups": lax.rem(scene + hop // n_tm, scenes)}
         return pltpu.make_async_remote_copy(
             src_ref=w_part(part, far_source(step)), dst_ref=w_part(part, far_source(step)),
             send_sem=wb_send.at[step, hop], recv_sem=wb_recv.at[step, hop],
-            device_id=column_peer(hop), device_id_type=MESH,
-        )
+            device_id=target, device_id_type=MESH,
+        )
+
+    def spread_send(step, hop):
+        return w_spread_copy(step, hop, column_source(hop % n_tm))
+
+    def spread_tm():
+        for step in range(1, chips):
+            w_far_copy(step, far_source(step)).wait_recv()
+            for hop in range(1, n_tm):
+                w_spread_copy(step, hop, column).start()
+            for other in range(1, scenes):
+                spread_send(step, other * n_tm).start()
+
+    def spread_groups():
+        for step in range(1, chips):
+            for hop in range(1, n_tm):
+                w_spread_copy(step, hop, column_source(hop)).wait_recv()
+                for other in range(1, scenes):
+                    spread_send(step, other * n_tm + hop).start()
 
     def w_forward_copy(step, hop, owner):
         part = column_source(hop)
@@ -171,11 +195,9 @@
         for step in range(1, chips):
             far_copy(g, step, tok).start()
         near_copy(g, tok).start()
-
-    for step in range(1, chips):
-        w_far_copy(step, far_source(step)).wait_recv()
-        for hop in range(1, columns):
-            w_spread_copy(step, hop, column).start()
+        if g == 1:
+            spread_tm()
+
     for part in range(columns):
         w_local_copy(part).start()
         w_near_copy(part, tok).start()
@@ -245,7 +267,7 @@
     def forward_weight():
         for step in range(1, chips):
             for hop in range(columns):
-                if hop:
+                if hop >= n_tm:
                     w_spread_copy(step, hop, column_source(hop)).wait_recv()
                 w_forward_copy(step, hop, far_source(step)).start()
 
@@ -258,35 +280,28 @@
                 source = lax.rem(chip + chips - step, chips) * 2 + (1 - core)
                 w_forward_copy(step, hop, source).wait_recv()
 
-    def store(r):
-        at = pl.ds(pl.multiple_of(r * tile, tile), tile)
-        return pltpu.make_async_copy(kbuf.at[at], out_hbm.at[0, at], out_sem.at[r])
+    def store(part):
+        cols = pl.ds(pl.multiple_of(part * w_cols, w_cols), w_cols)
+        return pltpu.make_async_copy(kbuf.at[:, cols], out_hbm.at[0, :, cols], out_sem.at[part])
 
     def project(low, high, first=False, last=False):
         depth = pl.ds(low * width, (high - low) * width)
 
-        def row_tile(r, _):
-            at = pl.ds(pl.multiple_of(r * tile, tile), tile)
-
-            def part_of(part, _):
-                cols = pl.ds(pl.multiple_of(part * w_cols, w_cols), w_cols)
-                total = jnp.dot(
-                    att[at, depth], weight[part, depth, :], preferred_element_type=jnp.float32
-                )
-                if not first:
-                    total = total + acc[at, cols]
-                if last:
-                    kbuf[at, cols] = total.astype(jnp.bfloat16)
-                else:
-                    acc[at, cols] = total
-                return 0
-
-            lax.fori_loop(0, columns, part_of, 0)
+        def part_of(part, _):
+            cols = pl.ds(pl.multiple_of(part * w_cols, w_cols), w_cols)
+            total = jnp.dot(
+                att[:, depth], weight[part, depth, :], preferred_element_type=jnp.float32
+            )
+            if not first:
+                total = total + acc[:, cols]
             if last:
-                store(r).start()
+                kbuf[:, cols] = total.astype(jnp.bfloat16)
+                store(part).start()
+            else:
+                acc[:, cols] = total
             return 0
 
-        lax.fori_loop(0, rows // tile, row_tile, 0)
+        lax.fori_loop(0, columns, part_of, 0)
 
     half = groups // 2
     for turn in range(groups + 2):
@@ -294,25 +309,30 @@
             frame_state(turn - 1)
         if 0 <= turn - 2 < groups:
             attend(turn - 2)
-        if turn == half:
+        if turn == 2:
+            spread_groups()
+        if turn == half + 1:
             forward_weight()
-        if turn == half + 1:
+        if turn == half + 2:
             await_weight()
             project(0, half, first=True)
-        if turn > half + 1:
+        if turn == half + 3:
+            project(half, half + 2)
+        if turn > half + 3:
             project(turn - 2, turn - 1, last=turn == groups + 1)
         if turn < groups:
             arrive(turn)
 
-    for r in range(rows // tile):
-        store(r).wait()
     for part in range(columns):
+        store(part).wait()
         w_near_copy(part, tok).wait_send()
     for step in range(1, chips):
         w_far_copy(step, tok).wait_send()
         for hop in range(columns):
-            if hop:
+            if 0 < hop < n_tm:
                 w_spread_copy(step, hop, column).wait_send()
+            elif hop:
+                spread_send(step, hop).wait_send()
             w_forward_copy(step, hop, far_source(step)).wait_send()
     for g in range(groups):
         near_copy(g, tok).wait_send()
@@ -372,7 +392,7 @@
             dma((groups, chips)),
             dma((groups, n_tm)),
             dma((groups, n_tm)),
-            dma((rows // min(rows, 256),)),
+            dma((columns,)),
             dma((columns,)),
             dma((columns,)),
             dma((columns,)),

time: 162 us -> 129 us (0.80); the launches traced: 159 us -> 129 us
  Pallas kernels: 152 us -> 121 us
    pallas_call x1, Pallas kernels: 152 us -> 121 us  [on_device(): pl.pallas_call(functools.partial(mix_kernel, n_tok, n_tm, columns, groups...]
where the time goes in v3:
time: 129 us
  Pallas kernels  121 us (94%)
  local copies, waits for them, and re-layouts  7.44 us (6%)
    pallas_call x1, Pallas kernels, on_device(): pl.pallas_call(functools.partial(mix_kernel, n_tok, n_tm, columns, groups...  121 us
    unnamed x2, local copies, waits for them, and re-layouts  6.16 us

profile of v3, /device:TPU:1, one launch (start us, length us, event | category | flops | bytes accessed | tf_op | source)
XLA Modules:
  0.0 128.9 jit_solution(13947741286860124268)
XLA Ops:
  0.0 1.4 %copy.7.index_ref = s32[1,32,12]{2,1,0:T(8,128)} copy(s32[1,32,12]{1,0,2:T(1,128)} %param.9) | data formatting | bytes 3072 | tf_op args[3]
  1.4 1.3 broadcast_in_dim.2.gain_in
  2.7 121.4 %shard_map.64 = bf16[1,1024,2048]{2,1,0:T(8,128)(2,1)} custom-call(s32[1,32,12]{2,1,0:T(8,128)} %copy.7.index_ref, f32[8,512]{1,0:T(8,128)} %broadcast_in_dim.2.gain_in, bf16[1,1024,2048]{2,1,0:T(8,128)(2,1)} %q_hbm.1, bf16[1,1024,2048]{2,1,0:T(8,128)(2,1)} %k_hbm.1, bf16[1,1024,2048]{2,1,0:T(8,128)(2,1)} %v_hbm.1, bf16[512,2048]{1,0:T(8,128)(2,1)} %w_hbm.1), custom_call_target="tpu_custom_call" | custom-call | flops 2147483648 | bytes 400000000 | tf_op jit(solution)/shard_map/pallas_call | solution.py:357
  124.1 4.8 %copy.9 = bf16[1,1024,2048]{2,1,0:T(8,128)(2,1)} copy(bf16[1,1024,2048]{2,1,0:T(8,128)(2,1)} %shard_map.64) | data formatting | bytes 8388608
